TPU v7x, 256 devices: a whole 4x4x8 slice. The times are simulated.
256 devices in a mesh: row: 8 (over z), col: 32 (over x, y, core).
Axes of the slice: x: 4, y: 4, z: 8, core: 2. Of those that a mesh axis runs over, the one named last changes fastest.
Arguments:
- embeddings: bfloat16 [49152, 256], P(('row', 'col')), may hold values from -256 to 256
- start_vectors: float32 [49152, 64], P(('row', 'col')), may hold values from -6 to 6
Outputs:
- spectral: float32 [49152, 64], P(('row', 'col'))
All inputs are finite; a program needn't handle non-finite values.
Results may differ from a plain program's by a relative error of at most 0.0068.
Values may be sent and summed in bfloat16 or wider, within the bound.
No kernel may reach another device: no remote copies, remote signals or barrier semaphores. Data moves between devices by JAX's collectives and lax.ppermute only.
A program may use at most 64 MiB of HBM per device.

v0:
```python
import math
import jax
import jax.numpy as jnp
from jax import lax
from jax.sharding import PartitionSpec as P

sharpness = 16.0
threshold = 0.3


def local(embeddings, start_vectors):
    local_docs = embeddings.shape[0]
    all_docs = local_docs * lax.axis_size("row") * lax.axis_size("col")
    widened = embeddings.astype(jnp.float32)
    unit_rows = (
        widened * lax.rsqrt(jnp.sum(widened * widened, axis=1, keepdims=True) + 1e-06)
    ).astype(jnp.bfloat16)
    column_set = lax.all_gather(unit_rows, "row", axis=0, tiled=True)
    scores = lax.dot_general(
        lax.all_gather(unit_rows, "col", axis=0, tiled=True),
        column_set,
        (((1,), (1,)), ((), ())),
        preferred_element_type=jnp.float32,
    )
    adjacency = jax.nn.sigmoid(sharpness * (scores - threshold)).astype(jnp.bfloat16)
    row_sums = jnp.sum(adjacency, axis=1, dtype=jnp.float32)
    degree_set = lax.psum(row_sums, "col")
    own_first = lax.axis_index("col") * local_docs
    degree = lax.dynamic_slice_in_dim(degree_set, own_first, local_docs, 0)
    inv_root = lax.rsqrt(degree)
    root_degree = jnp.sqrt(degree)

    def products(weighted):
        gathered = lax.all_gather(weighted, "row", axis=0, tiled=True)
        return (adjacency, gathered)

    def own_sums(weighted):
        tiles, gathered = products(weighted)
        return lax.psum_scatter(
            jnp.dot(tiles, gathered, preferred_element_type=jnp.float32),
            "col",
            scatter_dimension=0,
            tiled=True,
        )

    def deflation(vectors):
        return lax.psum(
            (jnp.sum(root_degree[:, None] * vectors, axis=0), jnp.sum(degree)), ("row", "col")
        )

    vectors = start_vectors
    weighted = (inv_root[:, None] * vectors).astype(jnp.bfloat16)
    correlation, degree_total = deflation(vectors)
    partial_sums = own_sums(weighted)
    vectors = (
        inv_root[:, None] * partial_sums
        - root_degree[:, None] * (correlation / degree_total)[None, :]
    )
    weighted = (inv_root[:, None] * vectors).astype(jnp.bfloat16)
    correlation, degree_total = deflation(vectors)
    partial_sums = own_sums(weighted)
    vectors = (
        inv_root[:, None] * partial_sums
        - root_degree[:, None] * (correlation / degree_total)[None, :]
    )
    gram_matrix = lax.psum(
        jnp.dot(vectors.T, vectors, precision=lax.Precision.HIGHEST), ("row", "col")
    )
    cholesky_factor = jnp.linalg.cholesky(gram_matrix)
    solved = lax.linalg.triangular_solve(cholesky_factor, vectors.T, left_side=True, lower=True)
    return solved.T * math.sqrt(all_docs)


def solution(mesh):
    return jax.shard_map(
        local,
        mesh=mesh,
        in_specs=(P(("row", "col"), None), P(("row", "col"), None)),
        out_specs=P(("row", "col"), None),
        check_vma=False,
    )
```

profile of v0, /device:TPU:1, one launch (start us, length us, event | category | flops | bytes accessed | tf_op | source)
XLA Modules:
  0.0 554.0 jit_solution(9075832216609413625)
XLA Ops:
  6.5 0.0 all-gather.4.cloned.1.call-start
  6.5 1.0 fusion
  7.6 1.6 fusion.1
  9.2 0.0 all-gather.4.cloned.1.call-update
  9.2 0.0 reduce-scatter.7.cloned.1.call-start
  9.2 24.6 %all_gather.13 = bf16[1536,256]{1,0:T(8,128)(2,1)S(1)} all-gather(bf16[192,256]{1,0:T(8,128)(2,1)} %fusion.1), channel_id=1, replica_groups=mesh['row'=8,'col'=32] {'row'}, dimensions={0}, use_global_device_ids=true | all-gather | bytes 884736 | tf_op jit(solution)/shard_map/all_gather | solution.py:18
  33.9 0.0 copy-start
  33.9 30.4 %all-gather.4.cloned.1.call-done = bf16[6144,256]{1,0:T(8,128)(2,1)} async-done(((bf16[192,256]{1,0:T(8,128)(2,1)}), bf16[6144,256]{1,0:T(8,128)(2,1)}) %all-gather.4.cloned.1.call-update) | async-done | bytes 3145744 | tf_op jit(solution)/shard_map/all_gather | solution.py:20
  64.2 16.3 %convert_reduce_fusion = (f32[6144]{0:T(1024)S(1)}, bf16[6144,1536]{0,1:T(8,128)(2,1)}) fusion(bf16[6144,256]{1,0:T(8,128)(2,1)} %all-gather.4.cloned.1.call-done, bf16[1536,256]{1,0:T(8,128)(2,1)S(1)} %all_gather.13), kind=kOutput, calls=%fused_computation | convolution fusion | flops 4907329536 | bytes 22831104 | tf_op jit(solution)/shard_map/dot_general | solution.py:19
  80.5 120.9 %psum.38 = f32[6144]{0:T(1024)S(1)} all-reduce(f32[6144]{0:T(1024)S(1)} %get-tuple-element.14), channel_id=1, replica_groups=mesh['row'=8,'col'=32] {'col'}, use_global_device_ids=true, to_apply=%region_2.0 | all-reduce | flops 6144 | bytes 49152 | tf_op jit(solution)/shard_map/psum | solution.py:27
  201.4 0.7 dynamic-slice_reduce_fusion
  202.0 0.0 copy-done
  202.1 0.1 multiply_reduce_fusion.1
  202.2 19.9 %all-gather = bf16[8,192,64]{1,2,0:T(8,128)(2,1)S(1)} all-gather(bf16[1,192,64]{1,2,0:T(8,128)(2,1)S(1)} %get-tuple-element.10), channel_id=1, replica_groups=mesh['row'=8,'col'=32] {'row'}, dimensions={0}, use_global_device_ids=true | all-gather | bytes 221184 | tf_op jit(solution)/shard_map/all_gather | solution.py:34
  222.1 0.1 copy.9
  222.2 0.2 reshape.20
  222.4 12.9 %fusion.14 = f32[6144,64]{1,0:T(8,128)} fusion(bf16[1536,64]{0,1:T(8,128)(2,1)S(1)} %reshape.20, bf16[6144,1536]{0,1:T(8,128)(2,1)} %get-tuple-element.15), kind=kOutput, calls=%fused_computation.37 | convolution fusion | flops 1207959552 | bytes 20643840
  235.4 0.0 reduce-scatter.7.cloned.1.call-update
  235.4 0.0 reduce-scatter.9.cloned.1.call-start
  235.5 83.2 %all-reduce = (f32[64]{0:T(128)S(1)}, f32[]{:T(128)}) all-reduce(f32[64]{0:T(128)S(1)} %get-tuple-element.9, f32[]{:T(128)} %get-tuple-element.11), channel_id=1, replica_groups=mesh['row'=8,'col'=32] {'row','col'}, use_global_device_ids=true, to_apply=%region_5.0 | all-reduce | flops 65 | bytes 520 | tf_op jit(solution)/shard_map/psum | solution.py:47
  318.7 0.6 broadcast_divide_fusion.1
  319.3 9.1 %reduce-scatter.7.cloned.1.call-done = f32[192,64]{1,0:T(8,128)} async-done(((f32[6144,64]{1,0:T(8,128)}), f32[192,64]{1,0:T(8,128)}) %reduce-scatter.7.cloned.1.call-update) | async-done | bytes 49168
  328.4 1.0 copy.15
  329.4 0.2 multiply_reduce_fusion
  329.5 20.3 %all-gather.1 = bf16[8,192,64]{1,2,0:T(8,128)(2,1)S(1)} all-gather(bf16[1,192,64]{1,2,0:T(8,128)(2,1)S(1)} %get-tuple-element.8), channel_id=1, replica_groups=mesh['row'=8,'col'=32] {'row'}, dimensions={0}, use_global_device_ids=true | all-gather | bytes 221184 | tf_op jit(solution)/shard_map/all_gather | solution.py:34
  349.8 0.1 copy.10
  350.0 0.2 reshape.22
  350.2 12.9 %fusion.15 = f32[6144,64]{1,0:T(8,128)} fusion(bf16[1536,64]{0,1:T(8,128)(2,1)S(1)} %reshape.22, bf16[6144,1536]{0,1:T(8,128)(2,1)} %get-tuple-element.15), kind=kOutput, calls=%fused_computation.38 | convolution fusion | flops 1207959552 | bytes 20643840
  363.2 0.0 reduce-scatter.9.cloned.1.call-update
  363.2 81.8 %psum.41 = f32[64]{0:T(128)S(1)} all-reduce(f32[64]{0:T(128)S(1)} %get-tuple-element.7), channel_id=1, replica_groups=mesh['row'=8,'col'=32] {'row','col'}, use_global_device_ids=true, to_apply=%region_10.0 | all-reduce | flops 64 | bytes 512 | tf_op jit(solution)/shard_map/psum | solution.py:47
  445.0 0.6 broadcast_divide_fusion
  445.7 10.1 %reduce-scatter.9.cloned.1.call-done = f32[192,64]{1,0:T(8,128)} async-done(((f32[6144,64]{1,0:T(8,128)}), f32[192,64]{1,0:T(8,128)}) %reduce-scatter.9.cloned.1.call-update) | async-done | bytes 49168
  455.8 1.0 copy.17
  456.8 0.3 fusion.2
  457.0 77.3 %psum.42 = f32[64,64]{0,1:T(8,128)S(1)} all-reduce(f32[64,64]{0,1:T(8,128)S(1)} %fusion.2), channel_id=1, replica_groups=mesh['row'=8,'col'=32] {'row','col'}, use_global_device_ids=true, to_apply=%region_11.0 | all-reduce | flops 4096 | bytes 32768 | tf_op jit(solution)/shard_map/psum | solution.py:66
  534.3 0.1 copy.12
  534.4 5.8 %cholesky.16 = f32[64,64]{1,0:T(8,128)S(1)} custom-call(f32[64,64]{1,0:T(8,128)S(1)} %fusion.7), custom_call_target="Cholesky" | custom-call | tf_op jit(solution)/shard_map/jit(cholesky)/cholesky | solution.py:69
  540.3 0.6 compare_reduce_fusion
  540.9 0.7 fusion.3
  541.6 4.9 custom-call.6
  546.5 0.9 convolution_multiply_fusion
  (3 shorter events, 0.0 us)
Async XLA Ops:
  6.5 57.7 %all-gather.4.cloned.1.call-start = ((), (), s32[]{:S(2)}) async-start(), calls=%async_computation.2 | async-start | bytes 3244032 | tf_op jit(solution)/shard_map/all_gather | solution.py:20
  9.2 319.2 %reduce-scatter.7.cloned.1.call-start = ((), (), s32[]{:S(2)}) async-start(), calls=%async_computation.3 | async-start | bytes 3244032
  33.9 168.2 %copy-start = (f32[192,64]{0,1:T(8,128)S(1)}, f32[192,64]{0,1:T(8,128)}, u32[]{:S(2)}) copy-start(f32[192,64]{0,1:T(8,128)} %param.3) | copy-start | bytes 147460
  235.4 220.4 %reduce-scatter.9.cloned.1.call-start = ((), (), s32[]{:S(2)}) async-start(), calls=%async_computation.4 | async-start | bytes 3244032
Sparse Core Ops, SparseCore 0:
  9.9 54.2 all-gather.3
  235.5 92.8 reduce-scatter.6
  363.3 92.4 reduce-scatter.8
where the time goes:
time: 555 us; the launch traced here: 554 us
  blocking collectives  428 us (77%)
  waiting for transfers between devices  49.6 us (9%)
  matrix products  43.3 us (8%)
  other arithmetic  17 us (3%)
  between operations  13.2 us (2%)
    psum x2, blocking collectives, deflation(): lax.psum((jnp.sum(root_degree[:, None] * vectors, axis=0), jnp.sum(degree...  165 us
    psum x1, blocking collectives, local(): degree_set = lax.psum(row_sums, 'col')  121 us
    psum x1, blocking collectives, local(): lax.psum(jnp.dot(vectors.T, vectors, precision=lax.Precision.HIGHEST), ('...  77.3 us
    all_gather x2, blocking collectives, products(): gathered = lax.all_gather(weighted, 'row', axis=0, tiled=True)  40.2 us
    all_gather x1, waiting for transfers between devices, local(): lax.all_gather(unit_rows, 'col', axis=0, tiled=True)  30.4 us
    unnamed x2, matrix products  25.9 us
    all_gather x1, blocking collectives, local(): column_set = lax.all_gather(unit_rows, 'row', axis=0, tiled=True)  24.6 us
    unnamed x5, waiting for transfers between devices  19.2 us
  transfers between devices with their start and end apart: 3, of which 3 were waited for; matrix products, arithmetic and copies ran while one was open for 0% of the time, Pallas kernels for 0%

commit v1 on v0

--- a/solution.py
+++ b/solution.py
@@ -63,8 +63,11 @@
         inv_root[:, None] * partial_sums
         - root_degree[:, None] * (correlation / degree_total)[None, :]
     )
-    gram_matrix = lax.psum(
-        jnp.dot(vectors.T, vectors, precision=lax.Precision.HIGHEST), ("row", "col")
+    gram_matrix = jnp.sum(
+        lax.all_gather(
+            jnp.dot(vectors.T, vectors, precision=lax.Precision.HIGHEST), ("row", "col")
+        ),
+        axis=0,
     )
     cholesky_factor = jnp.linalg.cholesky(gram_matrix)
     solved = lax.linalg.triangular_solve(cholesky_factor, vectors.T, left_side=True, lower=True)

time: 555 us -> 603 us (1.086)
  waiting for transfers between devices: 49.6 us -> 171 us
  blocking collectives: 428 us -> 351 us
    all_gather x0 -> x1, waiting for transfers between devices: none -> 121 us  [local(): lax.all_gather(jnp.dot(vectors.T, vectors, precision=lax.Precision.HIGHES...]
    psum x1 -> x0, blocking collectives: 77.3 us -> none  [local(): lax.psum(jnp.dot(vectors.T, vectors, precision=lax.Precision.HIGHEST), ('...]
    unnamed x5 -> x6, waiting for transfers between devices: 19.2 us -> 19.2 us
  transfers between devices with their start and end apart: 3 -> 4, of which waited for: 3 -> 4; matrix products, arithmetic and copies ran while one was open for 0% -> 0% of each run, Pallas kernels for 0% -> 0%
where the time goes in v1:
time: 603 us
  blocking collectives  351 us (58%)
  waiting for transfers between devices  171 us (28%)
  matrix products  44 us (7%)
  other arithmetic  21 us (3%)
  between operations  13.2 us (2%)
    psum x2, blocking collectives, deflation(): lax.psum((jnp.sum(root_degree[:, None] * vectors, axis=0), jnp.sum(degree...  165 us
    all_gather x1, waiting for transfers between devices, local(): lax.all_gather(jnp.dot(vectors.T, vectors, precision=lax.Precision.HIGHES...  121 us
    psum x1, blocking collectives, local(): degree_set = lax.psum(row_sums, 'col')  121 us
    all_gather x2, blocking collectives, products(): gathered = lax.all_gather(weighted, 'row', axis=0, tiled=True)  40.2 us
    all_gather x1, waiting for transfers between devices, local(): lax.all_gather(unit_rows, 'col', axis=0, tiled=True)  30.4 us
    unnamed x2, matrix products  25.9 us
    all_gather x1, blocking collectives, local(): column_set = lax.all_gather(unit_rows, 'row', axis=0, tiled=True)  24.6 us
    unnamed x6, waiting for transfers between devices  19.2 us
  transfers between devices with their start and end apart: 4, of which 4 were waited for; matrix products, arithmetic and copies ran while one was open for 0% of the time, Pallas kernels for 0%

profile of v1, /device:TPU:1, one launch (start us, length us, event | category | flops | bytes accessed | tf_op | source)
XLA Modules:
  0.0 602.7 jit_solution(8586219813445780514)
XLA Ops:
  6.5 0.0 all-gather.6.cloned.1.call-start
  6.5 1.0 fusion
  7.6 1.6 fusion.1
  9.2 0.0 all-gather.6.cloned.1.call-update
  9.2 0.0 reduce-scatter.7.cloned.1.call-start
  9.2 24.6 %all_gather.19 = bf16[1536,256]{1,0:T(8,128)(2,1)S(1)} all-gather(bf16[192,256]{1,0:T(8,128)(2,1)} %fusion.1), channel_id=1, replica_groups=mesh['row'=8,'col'=32] {'row'}, dimensions={0}, use_global_device_ids=true | all-gather | bytes 884736 | tf_op jit(solution)/shard_map/all_gather | solution.py:18
  33.9 0.0 copy-start
  33.9 30.4 %all-gather.6.cloned.1.call-done = bf16[6144,256]{1,0:T(8,128)(2,1)} async-done(((bf16[192,256]{1,0:T(8,128)(2,1)}), bf16[6144,256]{1,0:T(8,128)(2,1)}) %all-gather.6.cloned.1.call-update) | async-done | bytes 3145744 | tf_op jit(solution)/shard_map/all_gather | solution.py:20
  64.2 16.3 %convert_reduce_fusion = (f32[6144]{0:T(1024)S(1)}, bf16[6144,1536]{0,1:T(8,128)(2,1)}) fusion(bf16[6144,256]{1,0:T(8,128)(2,1)} %all-gather.6.cloned.1.call-done, bf16[1536,256]{1,0:T(8,128)(2,1)S(1)} %all_gather.19), kind=kOutput, calls=%fused_computation | convolution fusion | flops 4907329536 | bytes 22831104 | tf_op jit(solution)/shard_map/dot_general | solution.py:19
  80.5 120.9 %psum.31 = f32[6144]{0:T(1024)S(1)} all-reduce(f32[6144]{0:T(1024)S(1)} %get-tuple-element.14), channel_id=1, replica_groups=mesh['row'=8,'col'=32] {'col'}, use_global_device_ids=true, to_apply=%region_2.0 | all-reduce | flops 6144 | bytes 49152 | tf_op jit(solution)/shard_map/psum | solution.py:27
  201.4 0.7 dynamic-slice_reduce_fusion
  202.1 0.0 copy-done
  202.1 0.1 multiply_reduce_fusion.1
  202.2 19.9 %all-gather.1 = bf16[8,192,64]{1,2,0:T(8,128)(2,1)S(1)} all-gather(bf16[1,192,64]{1,2,0:T(8,128)(2,1)S(1)} %get-tuple-element.10), channel_id=1, replica_groups=mesh['row'=8,'col'=32] {'row'}, dimensions={0}, use_global_device_ids=true | all-gather | bytes 221184 | tf_op jit(solution)/shard_map/all_gather | solution.py:34
  222.1 0.1 copy.7
  222.2 0.2 reshape.21
  222.5 12.9 %fusion.14 = f32[6144,64]{1,0:T(8,128)} fusion(bf16[1536,64]{0,1:T(8,128)(2,1)S(1)} %reshape.21, bf16[6144,1536]{0,1:T(8,128)(2,1)} %get-tuple-element.15), kind=kOutput, calls=%fused_computation.37 | convolution fusion | flops 1207959552 | bytes 20643840
  235.4 0.0 reduce-scatter.7.cloned.1.call-update
  235.4 0.0 reduce-scatter.9.cloned.1.call-start
  235.5 83.2 %all-reduce = (f32[64]{0:T(128)S(1)}, f32[]{:T(128)}) all-reduce(f32[64]{0:T(128)S(1)} %get-tuple-element.9, f32[]{:T(128)} %get-tuple-element.11), channel_id=1, replica_groups=mesh['row'=8,'col'=32] {'row','col'}, use_global_device_ids=true, to_apply=%region_5.0 | all-reduce | flops 65 | bytes 520 | tf_op jit(solution)/shard_map/psum | solution.py:47
  318.7 0.6 broadcast_divide_fusion.1
  319.3 9.1 %reduce-scatter.7.cloned.1.call-done = f32[192,64]{1,0:T(8,128)} async-done(((f32[6144,64]{1,0:T(8,128)}), f32[192,64]{1,0:T(8,128)}) %reduce-scatter.7.cloned.1.call-update) | async-done | bytes 49168
  328.4 1.0 copy.11
  329.4 0.2 multiply_reduce_fusion
  329.5 20.3 %all-gather.2 = bf16[8,192,64]{1,2,0:T(8,128)(2,1)S(1)} all-gather(bf16[1,192,64]{1,2,0:T(8,128)(2,1)S(1)} %get-tuple-element.8), channel_id=1, replica_groups=mesh['row'=8,'col'=32] {'row'}, dimensions={0}, use_global_device_ids=true | all-gather | bytes 221184 | tf_op jit(solution)/shard_map/all_gather | solution.py:34
  349.8 0.1 copy.8
  350.0 0.2 reshape.23
  350.2 12.9 %fusion.15 = f32[6144,64]{1,0:T(8,128)} fusion(bf16[1536,64]{0,1:T(8,128)(2,1)S(1)} %reshape.23, bf16[6144,1536]{0,1:T(8,128)(2,1)} %get-tuple-element.15), kind=kOutput, calls=%fused_computation.38 | convolution fusion | flops 1207959552 | bytes 20643840
  363.2 0.0 reduce-scatter.9.cloned.1.call-update
  363.2 0.0 all-gather.8.cloned.1.call-start
  363.2 81.8 %psum.34 = f32[64]{0:T(128)S(1)} all-reduce(f32[64]{0:T(128)S(1)} %get-tuple-element.7), channel_id=1, replica_groups=mesh['row'=8,'col'=32] {'row','col'}, use_global_device_ids=true, to_apply=%region_10.0 | all-reduce | flops 64 | bytes 512 | tf_op jit(solution)/shard_map/psum | solution.py:47
  445.1 0.6 broadcast_divide_fusion
  445.7 10.1 %reduce-scatter.9.cloned.1.call-done = f32[192,64]{1,0:T(8,128)} async-done(((f32[6144,64]{1,0:T(8,128)}), f32[192,64]{1,0:T(8,128)}) %reduce-scatter.9.cloned.1.call-update) | async-done | bytes 49168
  455.8 1.0 copy.13
  456.8 0.9 fusion.2
  457.7 0.0 all-gather.8.cloned.1.call-update
  457.7 121.4 %all-gather.8.cloned.1.call-done = f32[16384,64]{1,0:T(8,128)} async-done(((f32[64,64]{1,0:T(8,128)}), f32[16384,64]{1,0:T(8,128)}) %all-gather.8.cloned.1.call-update) | async-done | bytes 4194320 | tf_op jit(solution)/shard_map/all_gather | solution.py:67
  579.1 4.0 reduce_sum.63
  583.1 0.1 copy.9
  583.2 5.8 cholesky.16
  589.1 0.6 compare_reduce_fusion
  589.7 0.7 fusion.3
  590.4 4.9 custom-call.6
  595.3 0.9 convolution_multiply_fusion
  (3 shorter events, 0.0 us)
Async XLA Ops:
  6.5 57.7 %all-gather.6.cloned.1.call-start = ((), (), s32[]{:S(2)}) async-start(), calls=%async_computation.2 | async-start | bytes 3244032 | tf_op jit(solution)/shard_map/all_gather | solution.py:20
  9.2 319.2 %reduce-scatter.7.cloned.1.call-start = ((), (), s32[]{:S(2)}) async-start(), calls=%async_computation.4 | async-start | bytes 3244032
  33.9 168.2 %copy-start = (f32[192,64]{0,1:T(8,128)S(1)}, f32[192,64]{0,1:T(8,128)}, u32[]{:S(2)}) copy-start(f32[192,64]{0,1:T(8,128)} %param.3) | copy-start | bytes 147460
  235.4 220.4 %reduce-scatter.9.cloned.1.call-start = ((), (), s32[]{:S(2)}) async-start(), calls=%async_computation.5 | async-start | bytes 3244032
  363.2 215.9 %all-gather.8.cloned.1.call-start = ((), (), s32[]{:S(2)}) async-start(), calls=%async_computation.3 | async-start | bytes 8421376 | tf_op jit(solution)/shard_map/all_gather | solution.py:67
Sparse Core Ops, SparseCore 0:
  9.9 54.2 all-gather.5
  235.5 92.8 reduce-scatter.6
  363.3 92.4 reduce-scatter.8
  459.4 119.6 all-gather.7

commit v2 on v0

--- a/solution.py
+++ b/solution.py
@@ -31,7 +31,14 @@
     root_degree = jnp.sqrt(degree)
 
     def products(weighted):
-        gathered = lax.all_gather(weighted, "row", axis=0, tiled=True)
+        ring = [weighted]
+        for hop in range(7):
+            ring.append(lax.ppermute(ring[-1], "row", [(dev, (dev + 1) % 8) for dev in range(8)]))
+        gathered = jnp.roll(
+            jnp.concatenate(ring[::-1], axis=0),
+            (lax.axis_index("row") + 1) * ring[0].shape[0],
+            axis=0,
+        )
         return (adjacency, gathered)
 
     def own_sums(weighted):

time: 555 us -> 577 us (1.040)
  waiting for transfers between devices: 49.6 us -> 106 us
  blocking collectives: 428 us -> 391 us
    ppermute x0 -> x14, waiting for transfers between devices: none -> 54.4 us  [products(): lax.ppermute(ring[-1], 'row', [(dev, (dev + 1) % 8) for dev in range(8)])]
    all_gather x2 -> x0, blocking collectives: 40.2 us -> none  [products(): gathered = lax.all_gather(weighted, 'row', axis=0, tiled=True)]
  transfers between devices with their start and end apart: 3 -> 17, of which waited for: 3 -> 17; matrix products, arithmetic and copies ran while one was open for 0% -> 0% of each run, Pallas kernels for 0% -> 0%
where the time goes in v2:
time: 577 us; the launch traced here: 576 us
  blocking collectives  391 us (68%)
  waiting for transfers between devices  106 us (18%)
  matrix products  43.9 us (8%)
  other arithmetic  17 us (3%)
  between operations  13.2 us (2%)
    psum x2, blocking collectives, deflation(): lax.psum((jnp.sum(root_degree[:, None] * vectors, axis=0), jnp.sum(degree...  169 us
    psum x1, blocking collectives, local(): degree_set = lax.psum(row_sums, 'col')  121 us
    psum x1, blocking collectives, local(): lax.psum(jnp.dot(vectors.T, vectors, precision=lax.Precision.HIGHEST), ('...  77.3 us
    ppermute x14, waiting for transfers between devices, products(): lax.ppermute(ring[-1], 'row', [(dev, (dev + 1) % 8) for dev in range(8)])  54.4 us
    all_gather x1, waiting for transfers between devices, local(): lax.all_gather(unit_rows, 'col', axis=0, tiled=True)  30.4 us
    unnamed x2, matrix products  26.3 us
    all_gather x1, blocking collectives, local(): column_set = lax.all_gather(unit_rows, 'row', axis=0, tiled=True)  24.6 us
    unnamed x5, waiting for transfers between devices  21.2 us
  transfers between devices with their start and end apart: 17, of which 17 were waited for; matrix products, arithmetic and copies ran while one was open for 0% of the time, Pallas kernels for 0%

profile of v2, /device:TPU:1, one launch (start us, length us, event | category | flops | bytes accessed | tf_op | source)
XLA Modules:
  0.0 576.4 jit_solution(11089118076547792525)
XLA Ops:
  6.5 1.0 fusion
  7.6 1.6 fusion.1
  9.2 0.0 reduce-scatter.7.cloned.1.call-start
  9.2 24.6 %all_gather.7 = bf16[1536,256]{1,0:T(8,128)(2,1)S(1)} all-gather(bf16[192,256]{1,0:T(8,128)(2,1)} %fusion.1), channel_id=1, replica_groups=mesh['row'=8,'col'=32] {'row'}, dimensions={0}, use_global_device_ids=true | all-gather | bytes 884736 | tf_op jit(solution)/shard_map/all_gather | solution.py:18
  33.9 30.4 %all-gather.2.cloned.1.call-done = bf16[6144,256]{1,0:T(8,128)(2,1)} async-done(((bf16[192,256]{1,0:T(8,128)(2,1)}), bf16[6144,256]{1,0:T(8,128)(2,1)}) %all-gather.2.cloned.1.call-update) | async-done | bytes 3145744 | tf_op jit(solution)/shard_map/all_gather | solution.py:20
  64.2 16.3 %convert_reduce_fusion = (f32[6144]{0:T(1024)S(1)}, bf16[6144,1536]{0,1:T(8,128)(2,1)}) fusion(bf16[6144,256]{1,0:T(8,128)(2,1)} %all-gather.2.cloned.1.call-done, bf16[1536,256]{1,0:T(8,128)(2,1)S(1)} %all_gather.7), kind=kOutput, calls=%fused_computation | convolution fusion | flops 4907329536 | bytes 22831104 | tf_op jit(solution)/shard_map/dot_general | solution.py:19
  80.6 120.9 %psum.38 = f32[6144]{0:T(1024)S(1)} all-reduce(f32[6144]{0:T(1024)S(1)} %get-tuple-element.15), channel_id=1, replica_groups=mesh['row'=8,'col'=32] {'col'}, use_global_device_ids=true, to_apply=%region_2.0 | all-reduce | flops 6144 | bytes 49152 | tf_op jit(solution)/shard_map/psum | solution.py:27
  201.4 0.7 dynamic-slice_reduce_fusion
  202.1 0.1 multiply_reduce_fusion.1
  202.2 1.3 collective-permute-start
  203.6 3.1 collective-permute-done
  206.7 4.0 collective-permute-done.1
  210.7 4.0 collective-permute-done.2
  214.6 4.0 collective-permute-done.3
  218.6 4.5 collective-permute-done.4
  223.1 4.0 collective-permute-done.5
  227.1 4.0 collective-permute-done.6
  231.1 0.1 concatenate.9
  231.2 13.2 %fusion.6 = f32[6144,64]{1,0:T(8,128)} fusion(bf16[6144,1536]{0,1:T(8,128)(2,1)} %get-tuple-element.16, s32[]{:T(128)S(6)} %select_n.22, bf16[1536,64]{0,1:T(8,128)(2,1)S(1)} %concatenate.9), kind=kOutput, calls=%fused_computation.14 | convolution fusion | flops 1208352768 | bytes 20643844
  244.4 0.0 reduce-scatter.7.cloned.1.call-update
  244.4 0.0 reduce-scatter.9.cloned.1.call-start
  244.4 84.4 %all-reduce = (f32[64]{0:T(128)S(1)}, f32[]{:T(128)}) all-reduce(f32[64]{0:T(128)S(1)} %get-tuple-element.10, f32[]{:T(128)} %get-tuple-element.12), channel_id=1, replica_groups=mesh['row'=8,'col'=32] {'row','col'}, use_global_device_ids=true, to_apply=%region_5.7 | all-reduce | flops 65 | bytes 520 | tf_op jit(solution)/shard_map/psum | solution.py:54
  328.9 0.6 broadcast_divide_fusion.1
  329.5 10.1 %reduce-scatter.7.cloned.1.call-done = f32[192,64]{1,0:T(8,128)} async-done(((f32[6144,64]{1,0:T(8,128)}), f32[192,64]{1,0:T(8,128)}) %reduce-scatter.7.cloned.1.call-update) | async-done | bytes 49168
  339.6 1.0 copy.9
  340.6 0.2 multiply_reduce_fusion
  340.8 1.3 collective-permute-start.7
  342.1 3.1 collective-permute-done.7
  345.2 4.0 collective-permute-done.8
  349.2 4.0 collective-permute-done.9
  353.2 4.0 collective-permute-done.10
  357.1 4.0 collective-permute-done.11
  361.1 4.0 collective-permute-done.12
  365.1 4.0 collective-permute-done.13
  369.1 0.1 concatenate.10
  369.2 13.2 %fusion.3 = f32[6144,64]{1,0:T(8,128)} fusion(bf16[6144,1536]{0,1:T(8,128)(2,1)} %get-tuple-element.16, s32[]{:T(128)S(6)} %select_n.22, bf16[1536,64]{0,1:T(8,128)(2,1)S(1)} %concatenate.10), kind=kOutput, calls=%fused_computation.12 | convolution fusion | flops 1208352768 | bytes 20643844
  382.4 84.1 %psum.41 = f32[64]{0:T(128)S(1)} all-reduce(f32[64]{0:T(128)S(1)} %get-tuple-element.8), channel_id=1, replica_groups=mesh['row'=8,'col'=32] {'row','col'}, use_global_device_ids=true, to_apply=%region_10.12 | all-reduce | flops 64 | bytes 512 | tf_op jit(solution)/shard_map/psum | solution.py:54
  466.5 0.6 broadcast_divide_fusion
  467.2 11.1 %reduce-scatter.9.cloned.1.call-done = f32[192,64]{1,0:T(8,128)} async-done(((f32[6144,64]{1,0:T(8,128)}), f32[192,64]{1,0:T(8,128)}) %reduce-scatter.9.cloned.1.call-update) | async-done | bytes 49168
  478.2 1.0 copy.11
  479.2 0.3 fusion.8
  479.5 77.3 %psum.42 = f32[64,64]{0,1:T(8,128)S(1)} all-reduce(f32[64,64]{0,1:T(8,128)S(1)} %fusion.8), channel_id=1, replica_groups=mesh['row'=8,'col'=32] {'row','col'}, use_global_device_ids=true, to_apply=%region_11.13 | all-reduce | flops 4096 | bytes 32768 | tf_op jit(solution)/shard_map/psum | solution.py:73
  556.7 0.1 copy.6
  556.8 5.8 %cholesky.16 = f32[64,64]{1,0:T(8,128)S(1)} custom-call(f32[64,64]{1,0:T(8,128)S(1)} %fusion.11), custom_call_target="Cholesky" | custom-call | tf_op jit(solution)/shard_map/jit(cholesky)/cholesky | solution.py:76
  562.7 0.6 compare_reduce_fusion
  563.4 0.7 fusion.9
  564.0 4.9 custom-call.6
  568.9 0.9 convolution_multiply_fusion
  (20 shorter events, 0.1 us)
Async XLA Ops:
  6.5 57.7 %all-gather.2.cloned.1.call-start = ((), (), s32[]{:S(2)}) async-start(), calls=%async_computation.2 | async-start | bytes 3244032 | tf_op jit(solution)/shard_map/all_gather | solution.py:20
  9.2 330.5 %reduce-scatter.7.cloned.1.call-start = ((), (), s32[]{:S(2)}) async-start(), calls=%async_computation.3 | async-start | bytes 3244032
  33.9 168.2 %copy-start = (f32[192,64]{0,1:T(8,128)S(1)}, f32[192,64]{0,1:T(8,128)}, u32[]{:S(2)}) copy-start(f32[192,64]{0,1:T(8,128)} %param.5) | copy-start | bytes 147460
  202.2 4.5 collective-permute-start
  206.7 4.0 collective-permute-start.1
  210.7 4.0 collective-permute-start.2
  214.6 4.0 collective-permute-start.3
  218.6 4.5 collective-permute-start.4
  223.1 4.0 collective-permute-start.5
  227.1 4.0 collective-permute-start.6
  244.4 233.8 %reduce-scatter.9.cloned.1.call-start = ((), (), s32[]{:S(2)}) async-start(), calls=%async_computation.4 | async-start | bytes 3244032
  340.8 4.4 collective-permute-start.7
  345.2 4.0 collective-permute-start.8
  349.2 4.0 collective-permute-start.9
  353.2 4.0 collective-permute-start.10
  357.1 4.0 collective-permute-start.11
  361.1 4.0 collective-permute-start.12
  365.1 4.0 collective-permute-start.13
Sparse Core Ops, SparseCore 0:
  9.9 54.2 all-gather.1
  244.5 95.0 reduce-scatter.6
  382.5 95.6 reduce-scatter.8
